TPU v7x, 32 devices: a whole 2x2x4 slice. The times are simulated.
32 devices in a mesh: grp: 2 (over core), dev: 16 (over z, y, x).
Axes of the slice: x: 2, y: 2, z: 4, core: 2. Of those that a mesh axis runs over, the one named last changes fastest.
Arguments:
- images: bfloat16 [16384, 64, 128], P(('grp', 'dev')), may hold values from -6 to 6
- test_maps: bfloat16 [64, 128, 32], replicated, may hold values from -6 to 6
- counts: int32 [64], replicated, may hold values from 24 to 64, as said below
Outputs:
- projected: bfloat16 [16384, 64, 32], P(('grp', 'dev'))
Inputs may be any that keep to these rules, and one draw needn't show every extreme that they name: `counts`: block 0 has 64 radial functions and block 63 has 24.
All inputs are finite; a program needn't handle non-finite values.
Results may differ from a plain program's by a relative error of at most 0.0049.
Values may be sent and summed in bfloat16 or wider, within the bound.
A program may use at most 64 MiB of HBM per device.

v0:
```python
import jax
import jax.numpy as jnp
from jax import lax
from jax.sharding import PartitionSpec as P


def orthonormal(summed):
    gram_matrix = jnp.einsum("krs,krt->kst", summed, summed, precision=lax.Precision.HIGHEST)
    factor = jnp.linalg.cholesky(gram_matrix)
    solved = lax.linalg.triangular_solve(
        factor, summed, left_side=False, lower=True, transpose_a=True
    )
    return solved.astype(jnp.bfloat16)


def body(images, test_maps, counts):
    columns = images.shape[2]
    radial = columns // 2
    position = lax.broadcasted_iota(jnp.int32, (images.shape[1], columns), 1) % radial
    valid_mask = (position < counts[:, None]).astype(jnp.bfloat16)
    masked = images * valid_mask[None]
    sketch = jnp.einsum(
        "ikr,krs->iks", masked, test_maps, preferred_element_type=jnp.float32
    ).astype(jnp.bfloat16)
    partial_sum = jnp.einsum("ikr,iks->krs", masked, sketch, preferred_element_type=jnp.float32)
    totals = lax.psum(partial_sum, "grp")
    owned = lax.psum_scatter(totals, "dev", scatter_dimension=0, tiled=True)
    basis_all = lax.all_gather(orthonormal(owned), "dev", axis=0, tiled=True)
    projected = jnp.einsum("ikr,krs->iks", masked, basis_all, preferred_element_type=jnp.float32)
    return projected.astype(jnp.bfloat16)


def solution(mesh):
    in_specs = (P(("grp", "dev"), None, None), P(), P())
    out_specs = P(("grp", "dev"), None, None)
    return jax.shard_map(body, mesh=mesh, in_specs=in_specs, out_specs=out_specs, check_vma=False)
```

profile of v0, /device:TPU:0, one launch (start us, length us, event | category | flops | bytes accessed | tf_op | source)
XLA Modules:
  0.0 233.2 jit_solution(13589502912707006677)
XLA Ops:
  6.5 0.0 copy-start
  6.5 0.0 reduce-scatter.2.cloned.1.call-start
  6.5 0.8 fusion.16
  7.3 7.2 %broadcast_multiply_fusion = bf16[512,64,128]{2,1,0:T(8,128)(2,1)} fusion(bf16[512,64,128]{2,1,0:T(8,128)(2,1)} %param.3, bf16[64,128]{1,0:T(8,128)(2,1)S(1)} %fusion.16), kind=kLoop, calls=%fused_computation.6 | loop fusion | flops 4194304 | bytes 16793600 | tf_op jit(solution)/shard_map/mul | solution.py:21
  14.5 0.0 copy-done
  14.5 24.3 %fusion.4 = f32[64,128,32]{1,2,0:T(8,128)} fusion(bf16[512,64,128]{2,1,0:T(8,128)(2,1)} %broadcast_multiply_fusion, bf16[64,128,32]{1,2,0:T(8,128)(2,1)S(1)} %copy-done), kind=kOutput, calls=%fused_computation.4 | convolution fusion | flops 537919488 | bytes 9961472 | tf_op jit(solution)/shard_map/ikr,iks->krs/dot_general | solution.py:25
  38.8 0.0 reduce-scatter.2.cloned.1.call-update
  38.8 0.0 all-reduce.2.cloned.1.call-start
  38.9 80.5 %reduce-scatter.2.cloned.1.call-done = f32[4,128,32]{1,2,0:T(8,128)} async-done(((f32[64,128,32]{1,2,0:T(8,128)}), f32[4,128,32]{1,2,0:T(8,128)}) %reduce-scatter.2.cloned.1.call-update) | async-done | bytes 65552 | tf_op jit(solution)/shard_map/reduce_scatter | solution.py:27
  119.4 0.0 all-reduce.2.cloned.1.call-update
  119.4 16.7 %all-reduce.2.cloned.1.call-done = f32[4,128,32]{1,2,0:T(8,128)} async-done(((f32[4,128,32]{1,2,0:T(8,128)}), f32[4,128,32]{1,2,0:T(8,128)}) %all-reduce.2.cloned.1.call-update) | async-done | bytes 65552 | tf_op jit(solution)/shard_map/psum | solution.py:26
  136.2 1.1 fusion.17
  137.3 0.1 copy.12
  137.4 11.7 %custom-call.7 = f32[4,32,32]{2,1,0:T(8,128)S(1)} custom-call(f32[4,32,32]{2,1,0:T(8,128)S(1)} %fusion.15), custom_call_target="Cholesky" | custom-call | tf_op jit(solution)/shard_map/jit(cholesky)/cholesky | solution.py:9
  149.2 0.1 compare_reduce_fusion
  149.3 0.1 select_bitcast_fusion
  149.4 9.8 %custom-call.8 = f32[4,1,32,32]{2,3,1,0:T(8,128)S(1)} custom-call(f32[4,1,32,32]{3,2,1,0:T(8,128)S(1)} %select_bitcast_fusion), custom_call_target="InvertDiagBlocksLowerTriangular" | custom-call | tf_op jit(solution)/shard_map/triangular_solve | solution.py:10
  159.2 1.2 convolution_convert_fusion
  160.4 44.2 %all_gather.3 = bf16[64,128,32]{1,2,0:T(8,128)(2,1)S(1)} all-gather(bf16[4,128,32]{1,2,0:T(8,128)(2,1)S(1)} %convolution_convert_fusion), channel_id=1, replica_groups=mesh['grp'=2,'dev'=16] {'dev'}, dimensions={0}, use_global_device_ids=true | all-gather | bytes 557056 | tf_op jit(solution)/shard_map/all_gather | solution.py:28
  204.6 21.8 %convert_bitcast_fusion = bf16[512,64,32]{0,2,1:T(8,128)(2,1)} fusion(bf16[64,128,32]{1,2,0:T(8,128)(2,1)S(1)} %all_gather.3, bf16[512,64,128]{2,1,0:T(8,128)(2,1)} %broadcast_multiply_fusion), kind=kOutput, calls=%fused_computation.8 | convolution fusion | flops 269484032 | bytes 11010048 | tf_op jit(solution)/shard_map/ikr,krs->iks/dot_general | solution.py:29
  (6 shorter events, 0.1 us)
Async XLA Ops:
  6.5 8.0 %copy-start = (bf16[64,128,32]{1,2,0:T(8,128)(2,1)S(1)}, bf16[64,128,32]{1,2,0:T(8,128)(2,1)}, u32[]{:S(2)}) copy-start(bf16[64,128,32]{1,2,0:T(8,128)(2,1)} %param.4) | copy-start | bytes 1572868
  6.5 112.9 %reduce-scatter.2.cloned.1.call-start = ((), (), s32[]{:S(2)}) async-start(), calls=%async_computation.1 | async-start | bytes 1114112 | tf_op jit(solution)/shard_map/reduce_scatter | solution.py:27
  38.8 97.3 %all-reduce.2.cloned.1.call-start = ((), (), s32[]{:S(2)}) async-start(), calls=%async_computation.2 | async-start | bytes 131072 | tf_op jit(solution)/shard_map/psum | solution.py:26
Sparse Core Ops, SparseCore 0:
  39.0 80.4 reduce-scatter.1
  121.8 14.3 all-reduce.1
where the time goes:
time: 234 us; the launch traced here: 233 us
  waiting for transfers between devices  97.3 us (42%)
  matrix products  48.4 us (21%)
  blocking collectives  44.2 us (19%)
  other arithmetic  29.8 us (13%)
  between operations  13.4 us (6%)
    reduce_scatter x1, waiting for transfers between devices, body(): owned = lax.psum_scatter(totals, 'dev', scatter_dimension=0, tiled=True)  80.5 us
    all_gather x1, blocking collectives, body(): basis_all = lax.all_gather(orthonormal(owned), 'dev', axis=0, tiled=True)  44.2 us
    dot_general x1, matrix products, body(): jnp.einsum('ikr,iks->krs', masked, sketch, preferred_element_type=jnp.flo...  24.3 us
    dot_general x1, matrix products, body(): jnp.einsum('ikr,krs->iks', masked, basis_all, preferred_element_type=jnp....  21.8 us
    psum x1, waiting for transfers between devices, body(): totals = lax.psum(partial_sum, 'grp')  16.7 us
    another operation x4, other arithmetic, orthonormal(): factor = jnp.linalg.cholesky(gram_matrix)  11.9 us
    another operation x3, other arithmetic, orthonormal(): lax.linalg.triangular_solve(factor, summed, left_side=False, lower=True,...  9.94 us
    mul x1, other arithmetic, body(): masked = images * valid_mask[None]  7.16 us
  transfers between devices with their start and end apart: 2, of which 2 were waited for; matrix products, arithmetic and copies ran while one was open for 0% of the time, Pallas kernels for 0%

commit v1 on v0

v1 whole, which is shorter than its diff:
```python
import functools

import jax
import jax.numpy as jnp
from jax import lax
from jax.experimental import pallas as pl
from jax.experimental.pallas import tpu as pltpu
from jax.sharding import PartitionSpec as P

MESH = pl.DeviceIdType.MESH


def orthonormal(summed):
    gram_matrix = jnp.einsum("krs,krt->kst", summed, summed, precision=lax.Precision.HIGHEST)
    factor = jnp.linalg.cholesky(gram_matrix)
    solved = lax.linalg.triangular_solve(
        factor, summed, left_side=False, lower=True, transpose_a=True
    )
    return solved.astype(jnp.bfloat16)


def basis_kernel(groups, devs, part_ref, out_ref, pair, half, slots, work, gath,
                 pair_send, pair_recv, sum_send, sum_recv, all_send, all_recv,
                 share_send, share_recv):
    me_g, me_d = lax.axis_index("grp"), lax.axis_index("dev")
    blocks, rank, columns = part_ref.shape
    per_group = blocks // groups
    own = per_group // devs

    barrier = pltpu.get_barrier_semaphore()
    for step in range(1, groups):
        pl.semaphore_signal(barrier, inc=1, device_id=((me_g + step) % groups, me_d), device_id_type=MESH)

    @pl.loop(1, devs)
    def _(step):
        pl.semaphore_signal(barrier, inc=1, device_id=(me_g, (me_d + step) % devs), device_id_type=MESH)

    pl.semaphore_wait(barrier, groups - 1 + devs - 1)

    pair_copies = []
    for step in range(1, groups):
        peer = (me_g + step) % groups
        copy = pltpu.make_async_remote_copy(
            src_ref=part_ref.at[pl.ds(peer * per_group, per_group)],
            dst_ref=pair.at[step - 1],
            send_sem=pair_send.at[step - 1],
            recv_sem=pair_recv.at[step - 1],
            device_id=(peer, me_d),
            device_id_type=MESH,
        )
        copy.start()
        pair_copies.append(copy)
    for copy in pair_copies:
        copy.wait()

    @pl.loop(0, per_group)
    def _(b):
        value = part_ref[me_g * per_group + b]
        for step in range(1, groups):
            value += pair[step - 1, b]
        half[b] = value

    def to_owner(step):
        target = (me_d + step) % devs
        return pltpu.make_async_remote_copy(
            src_ref=half.at[pl.ds(target * own, own)],
            dst_ref=slots.at[step],
            send_sem=sum_send.at[step],
            recv_sem=sum_recv.at[step],
            device_id=(me_g, target),
            device_id_type=MESH,
        )

    @pl.loop(1, devs)
    def _(step):
        to_owner(step).start()

    work[...] = half[pl.ds(me_d * own, own)]

    @pl.loop(1, devs)
    def _(step):
        to_owner(step).wait()
        work[...] += slots[step]

    position = lax.broadcasted_iota(jnp.int32, (own, rank, columns), 1)

    @pl.loop(0, rank)
    def _(j):
        rows = work[...]
        row = work[:, pl.ds(j, 1), :]
        along = jnp.sum(rows * row, axis=2, keepdims=True)
        scale = lax.rsqrt(jnp.sum(row * row, axis=2, keepdims=True))
        unit = row * scale
        later = rows - (along * scale) * unit
        work[...] = jnp.where(position > j, later, jnp.where(position == j, jnp.broadcast_to(unit, rows.shape), rows))

    mine = me_g * per_group + me_d * own
    gath[pl.ds(mine, own)] = work[...].astype(gath.dtype)

    def to_all(step):
        return pltpu.make_async_remote_copy(
            src_ref=gath.at[pl.ds(mine, own)],
            dst_ref=gath.at[pl.ds(mine, own)],
            send_sem=all_send.at[step],
            recv_sem=all_recv.at[step],
            device_id=(me_g, (me_d + step) % devs),
            device_id_type=MESH,
        )

    @pl.loop(1, devs)
    def _(step):
        to_all(step).start()

    @pl.loop(1, devs)
    def _(step):
        to_all(step).wait()

    share_copies = []
    for step in range(1, groups):
        part = gath.at[pl.ds(me_g * per_group, per_group)]
        copy = pltpu.make_async_remote_copy(
            src_ref=part,
            dst_ref=part,
            send_sem=share_send.at[step - 1],
            recv_sem=share_recv.at[step - 1],
            device_id=((me_g + step) % groups, me_d),
            device_id_type=MESH,
        )
        copy.start()
        share_copies.append(copy)
    for copy in share_copies:
        copy.wait()

    @pl.loop(0, blocks)
    def _(b):
        out_ref[b] = gath[b]


def all_bases(groups, devs, partial):
    blocks, rank, columns = partial.shape
    per_group = blocks // groups
    own = per_group // devs
    dma = pltpu.SemaphoreType.DMA
    return pl.pallas_call(
        functools.partial(basis_kernel, groups, devs),
        out_shape=jax.ShapeDtypeStruct(partial.shape, jnp.bfloat16),
        in_specs=[pl.BlockSpec(memory_space=pltpu.VMEM)],
        out_specs=pl.BlockSpec(memory_space=pltpu.VMEM),
        scratch_shapes=[
            pltpu.VMEM((groups - 1, per_group, rank, columns), jnp.float32),
            pltpu.VMEM((per_group, rank, columns), jnp.float32),
            pltpu.VMEM((devs, own, rank, columns), jnp.float32),
            pltpu.VMEM((own, rank, columns), jnp.float32),
            pltpu.VMEM(partial.shape, jnp.bfloat16),
            dma((groups - 1,)),
            dma((groups - 1,)),
            dma((devs,)),
            dma((devs,)),
            dma((devs,)),
            dma((devs,)),
            dma((groups - 1,)),
            dma((groups - 1,)),
        ],
        compiler_params=pltpu.CompilerParams(
            collective_id=0, has_side_effects=True, vmem_limit_bytes=24 * 1024 * 1024
        ),
    )(partial)


def body(groups, devs, images, test_maps, counts):
    blocks, columns = images.shape[1:]
    radial = columns // 2
    position = lax.broadcasted_iota(jnp.int32, (blocks, columns), 1) % radial
    valid = position < counts[:, None]
    maps = jnp.where(valid[:, :, None], test_maps, jnp.zeros_like(test_maps))
    sketch = jnp.einsum(
        "ikr,krs->iks", images, maps, preferred_element_type=jnp.float32
    ).astype(jnp.bfloat16)
    if groups > 1 and devs > 1 and blocks % (groups * devs) == 0:
        partial = jnp.einsum("ikr,iks->ksr", images, sketch, preferred_element_type=jnp.float32)
        partial = jnp.where(valid[:, None, :], partial, 0.0)
        basis_all = all_bases(groups, devs, partial)
        projected = jnp.einsum("ikr,ksr->iks", images, basis_all, preferred_element_type=jnp.float32)
    else:
        partial = jnp.einsum("ikr,iks->krs", images, sketch, preferred_element_type=jnp.float32)
        partial = jnp.where(valid[:, :, None], partial, 0.0)
        totals = lax.psum(partial, "grp")
        owned = lax.psum_scatter(totals, "dev", scatter_dimension=0, tiled=True)
        basis_all = lax.all_gather(orthonormal(owned), "dev", axis=0, tiled=True)
        projected = jnp.einsum("ikr,krs->iks", images, basis_all, preferred_element_type=jnp.float32)
    return projected.astype(jnp.bfloat16)


def solution(mesh):
    in_specs = (P(("grp", "dev"), None, None), P(), P())
    out_specs = P(("grp", "dev"), None, None)
    part = functools.partial(body, mesh.shape["grp"], mesh.shape["dev"])
    return jax.shard_map(part, mesh=mesh, in_specs=in_specs, out_specs=out_specs, check_vma=False)
```

time: 234 us -> 77.8 us (0.33)
  waiting for transfers between devices: 97.3 us -> 0 us
  blocking collectives: 44.2 us -> 0 us
  Pallas kernels: 0 us -> 33.4 us
  other arithmetic: 29.8 us -> 0.74 us
  between operations: 13.4 us -> 0.02 us
  matrix products: 48.4 us -> 43.5 us
    reduce_scatter x1 -> x0, waiting for transfers between devices: 80.5 us -> none  [body(): owned = lax.psum_scatter(totals, 'dev', scatter_dimension=0, tiled=True)]
    all_gather x1 -> x0, blocking collectives: 44.2 us -> none  [body(): basis_all = lax.all_gather(orthonormal(owned), 'dev', axis=0, tiled=True)]
    pallas_call x0 -> x1, Pallas kernels: none -> 33.4 us  [all_bases(): pl.pallas_call(functools.partial(basis_kernel, groups, devs), out_shape=j...]
    another operation x7 -> x0, other arithmetic: 21.8 us -> none  [the longest x4 11.9 us: orthonormal(): factor = jnp.linalg.cholesky(gram_matrix)]
    psum x1 -> x0, waiting for transfers between devices: 16.7 us -> none  [body(): totals = lax.psum(partial_sum, 'grp')]
    mul x1 -> x0, other arithmetic: 7.16 us -> none  [body(): masked = images * valid_mask[None]]
    dot_general x3 -> x2, matrix products: 47.2 us -> 43.5 us  [the longest x1 21.8 us: body(): jnp.einsum('ikr,ksr->iks', images, basis_all, preferred_element_type=jnp....]
  transfers between devices with their start and end apart: 2 -> 0, of which waited for: 2 -> 0; matrix products, arithmetic and copies ran while one was open for 0% -> 0% of each run, Pallas kernels for 0% -> 0%
where the time goes in v1:
time: 77.8 us; the launch traced here: 77.7 us
  matrix products  43.5 us (56%)
  Pallas kernels  33.4 us (43%)
    pallas_call x1, Pallas kernels, all_bases(): pl.pallas_call(functools.partial(basis_kernel, groups, devs), out_shape=j...  33.4 us
    dot_general x1, matrix products, body(): jnp.einsum('ikr,ksr->iks', images, basis_all, preferred_element_type=jnp....  21.8 us
    dot_general x1, matrix products, body(): jnp.einsum('ikr,iks->ksr', images, sketch, preferred_element_type=jnp.flo...  21.7 us

profile of v1, /device:TPU:0, one launch (start us, length us, event | category | flops | bytes accessed | tf_op | source)
XLA Modules:
  0.0 77.7 jit_solution(3979412323217869156)
XLA Ops:
  0.0 0.7 select_compare_fusion
  0.7 21.7 %fusion.14.part_ref = f32[64,32,128]{2,1,0:T(8,128)S(1)} fusion(bf16[512,64,128]{2,1,0:T(8,128)(2,1)} %param.3, bf16[64,128,32]{1,2,0:T(8,128)(2,1)} %param.4, pred[64,128]{1,0:T(8,128)(4,1)S(1)} %select_compare_fusion), kind=kOutput, calls=%fused_computation.9 | convolution fusion | flops 538443776 | bytes 9969664 | tf_op jit(solution)/shard_map/ikr,iks->ksr/dot_general | solution.py:180
  22.4 33.4 %shard_map.37 = bf16[64,32,128]{2,1,0:T(8,128)(2,1)S(1)} custom-call(f32[64,32,128]{2,1,0:T(8,128)S(1)} %fusion.14.part_ref), custom_call_target="tpu_custom_call" | custom-call | tf_op jit(solution)/shard_map/pallas_call | solution.py:144
  55.9 21.8 %convert_bitcast_fusion = bf16[512,64,32]{0,2,1:T(8,128)(2,1)} fusion(bf16[64,32,128]{2,1,0:T(8,128)(2,1)S(1)} %shard_map.37, bf16[512,64,128]{2,1,0:T(8,128)(2,1)} %param.3), kind=kOutput, calls=%fused_computation.7 | convolution fusion | flops 269484032 | bytes 11010048 | tf_op jit(solution)/shard_map/ikr,ksr->iks/dot_general | solution.py:183
  (2 shorter events, 0.0 us)

commit v2 on v1

--- a/solution.py
+++ b/solution.py
@@ -4,6 +4,7 @@
 import jax.numpy as jnp
 from jax import lax
 from jax.experimental import pallas as pl
+from jax.experimental.layout import Layout, with_layout_constraint
 from jax.experimental.pallas import tpu as pltpu
 from jax.sharding import PartitionSpec as P
 
@@ -173,15 +174,21 @@
     position = lax.broadcasted_iota(jnp.int32, (blocks, columns), 1) % radial
     valid = position < counts[:, None]
     maps = jnp.where(valid[:, :, None], test_maps, jnp.zeros_like(test_maps))
-    sketch = jnp.einsum(
-        "ikr,krs->iks", images, maps, preferred_element_type=jnp.float32
-    ).astype(jnp.bfloat16)
     if groups > 1 and devs > 1 and blocks % (groups * devs) == 0:
-        partial = jnp.einsum("ikr,iks->ksr", images, sketch, preferred_element_type=jnp.float32)
+        by_block = with_layout_constraint(images.transpose(1, 0, 2), Layout((0, 1, 2)))
+        by_block = lax.optimization_barrier(by_block)
+        sketch = jnp.einsum(
+            "kir,krs->ksi", by_block, maps, preferred_element_type=jnp.float32
+        ).astype(jnp.bfloat16)
+        partial = jnp.einsum("kir,ksi->ksr", by_block, sketch, preferred_element_type=jnp.float32)
         partial = jnp.where(valid[:, None, :], partial, 0.0)
         basis_all = all_bases(groups, devs, partial)
-        projected = jnp.einsum("ikr,ksr->iks", images, basis_all, preferred_element_type=jnp.float32)
+        projected = jnp.einsum("kir,ksr->ksi", by_block, basis_all, preferred_element_type=jnp.float32)
+        return projected.astype(jnp.bfloat16).transpose(2, 0, 1)
     else:
+        sketch = jnp.einsum(
+            "ikr,krs->iks", images, maps, preferred_element_type=jnp.float32
+        ).astype(jnp.bfloat16)
         partial = jnp.einsum("ikr,iks->krs", images, sketch, preferred_element_type=jnp.float32)
         partial = jnp.where(valid[:, :, None], partial, 0.0)
         totals = lax.psum(partial, "grp")

time: 77.8 us -> 63.7 us (0.82)
  matrix products: 43.5 us -> 17.5 us
  local copies, waits for them, and re-layouts: 0 us -> 12.1 us
    dot_general x2, matrix products: 43.5 us -> 17.5 us  [the longest x1 9.83 us: body(): jnp.einsum('kir,ksi->ksr', by_block, sketch, preferred_element_type=jnp.f...]
    unnamed x0 -> x3, local copies, waits for them, and re-layouts: none -> 12.1 us
where the time goes in v2:
time: 63.7 us; the launch traced here: 63.6 us
  Pallas kernels  33.3 us (52%)
  matrix products  17.5 us (27%)
  local copies, waits for them, and re-layouts  12.1 us (19%)
  other arithmetic  0.74 us (1%)
    pallas_call x1, Pallas kernels, all_bases(): pl.pallas_call(functools.partial(basis_kernel, groups, devs), out_shape=j...  33.3 us
    unnamed x3, local copies, waits for them, and re-layouts  12.1 us
    dot_general x1, matrix products, body(): jnp.einsum('kir,ksi->ksr', by_block, sketch, preferred_element_type=jnp.f...  9.83 us
    dot_general x1, matrix products, body(): jnp.einsum('kir,ksr->ksi', by_block, basis_all, preferred_element_type=jn...  7.68 us

profile of v2, /device:TPU:0, one launch (start us, length us, event | category | flops | bytes accessed | tf_op | source)
XLA Modules:
  0.0 63.6 jit_solution(14838992201120983783)
XLA Ops:
  0.0 0.7 %select_compare_fusion = pred[64,128]{1,0:T(8,128)(4,1)S(1)} fusion(s32[64]{0:T(128)} %param.5, s32[128]{0:T(128)S(1)} %get-tuple-element.5, s32[128]{0:T(128)S(1)} %get-tuple-element.6, pred[128]{0:T(512)(128)(4,1)S(1)} %compare_and_fusion), kind=kLoop, calls=%fused_computation.9 | loop fusion | flops 16384 | bytes 9600 | tf_op jit(solution)/shard_map/lt | solution.py:175
  0.7 0.0 copy-start
  0.8 12.0 %copy.6 = bf16[512,64,128]{2,0,1:T(8,128)(2,1)} copy(bf16[512,64,128]{2,1,0:T(8,128)(2,1)} %param.3) | data formatting | bytes 16777216 | tf_op args[0]
  12.8 0.0 copy-done
  12.8 9.8 %fusion.4.part_ref = f32[64,32,128]{2,1,0:T(8,128)S(1)} fusion(bf16[64,512,128]{2,1,0:T(8,128)(2,1)} %bitcast.9, bf16[64,128,32]{1,2,0:T(8,128)(2,1)S(1)} %copy-done, pred[64,128]{1,0:T(8,128)(4,1)S(1)} %select_compare_fusion), kind=kOutput, calls=%fused_computation.5 | convolution fusion | flops 538443776 | bytes 9969664 | tf_op jit(solution)/shard_map/kir,ksi->ksr/dot_general | solution.py:183
  22.6 33.3 %shard_map.37 = bf16[64,32,128]{2,1,0:T(8,128)(2,1)S(1)} custom-call(f32[64,32,128]{2,1,0:T(8,128)S(1)} %fusion.4.part_ref), custom_call_target="tpu_custom_call" | custom-call | tf_op jit(solution)/shard_map/pallas_call | solution.py:145
  55.9 7.7 %convert_bitcast_fusion = bf16[512,64,32]{0,2,1:T(8,128)(2,1)} fusion(bf16[64,32,128]{2,1,0:T(8,128)(2,1)S(1)} %shard_map.37, bf16[64,512,128]{2,1,0:T(8,128)(2,1)} %bitcast.10), kind=kOutput, calls=%fused_computation.1 | convolution fusion | flops 269484032 | bytes 11010048 | tf_op jit(solution)/shard_map/kir,ksr->ksi/dot_general | solution.py:186
  (2 shorter events, 0.0 us)
Async XLA Ops:
  0.7 12.1 %copy-start = (bf16[64,128,32]{1,2,0:T(8,128)(2,1)S(1)}, bf16[64,128,32]{1,2,0:T(8,128)(2,1)}, u32[]{:S(2)}) copy-start(bf16[64,128,32]{1,2,0:T(8,128)(2,1)} %param.4) | copy-start | bytes 1572868
